TPU v7x, 32 devices: a whole 2x2x4 slice. The times are simulated.
32 devices in a mesh: grp: 2 (over x), row: 2 (over core), col: 8 (over z, y).
Axes of the slice: x: 2, y: 2, z: 4, core: 2. Of those that a mesh axis runs over, the one named last changes fastest.
Arguments:
- tokens: bfloat16 [256, 4096], P(('grp', 'col'), 'row'), parts along dimension 0, may hold values from -6 to 6
- cotangent: bfloat16 [256, 4096], P(('grp', 'col'), 'row'), parts along dimension 0, may hold values from -6 to 6
- adapter_index: int32 [256], P('grp'), parts along dimension 0, may hold values from 0 to 7
- retain_mask: int32 [3, 224, 64], P(None, 'col', 'row'), may hold values 0 or 1
- gate_weight: bfloat16 [14336, 4096], P('col', 'row'), may hold values from -0.09375 to 0.09375
- up_weight: bfloat16 [14336, 4096], P('col', 'row'), may hold values from -0.09375 to 0.09375
- down_weight: bfloat16 [14336, 4096], P('col', 'row'), may hold values from -0.046875 to 0.046875
- adapter_up_input: bfloat16 [4096, 256], P('row'), may hold values from -0.09375 to 0.09375
- adapter_up_output: bfloat16 [256, 14336], P(None, 'col'), may hold values from -0.125 to 0.125
- adapter_down_input: bfloat16 [14336, 256], P('col'), may hold values from -0.046875 to 0.046875
- adapter_down_output: bfloat16 [256, 4096], P(None, 'row'), may hold values from -0.25 to 0.25
Outputs:
- layer_output: bfloat16 [256, 4096], P(('grp', 'col'), 'row'), parts along dimension 0
- token_gradient: bfloat16 [256, 4096], P(('grp', 'col'), 'row'), parts along dimension 0
- grad_up_in: bfloat16 [8192, 256], P(('grp', 'row')), parts along dimension 0
- grad_up_out: bfloat16 [512, 14336], P('grp', 'col'), parts along dimension 0
- grad_down_in: bfloat16 [28672, 256], P(('grp', 'col')), parts along dimension 0
- grad_down_out: bfloat16 [512, 4096], P('grp', 'row'), parts along dimension 0
There are 2 independent parts, one for each index of `grp`. A program takes and returns all parts, laid end to end along the dimension named above; an argument that names none is the same for every part. Nothing has to cross between parts.
All inputs are finite; a program needn't handle non-finite values. No bound on the sum of `retain_mask` on one device may be relied on, other than what follows from the above.
Results may differ from a plain program's by a relative error of at most 0.02.
Values may be sent and summed in bfloat16 or wider, within the bound.
A program may use at most 192 MiB of HBM per device.

v0:
```python
import jax
import jax.numpy as jnp
from jax import lax
from jax.sharding import PartitionSpec as P

BLOCK = 64
REWARD_ADAPTERS = 8
ADAPTER_RANK = 32


def pruned(weight, retain_mask, which):
    grid = retain_mask[which].astype(jnp.bfloat16)
    unit_rows, model_cols = weight.shape
    tiles = weight.reshape(unit_rows // BLOCK, BLOCK, model_cols // BLOCK, BLOCK)
    return (tiles * grid[:, None, :, None]).reshape(unit_rows, model_cols)


def hidden_update(
    gate_signal,
    up_frozen,
    lowrank_up,
    frozen_gradient,
    lowrank_down,
    member_choose,
    adapter_up_output,
    adapter_down_input,
):
    up_lowrank = (member_choose * lowrank_up).astype(jnp.bfloat16)
    up_activation = up_frozen + jnp.dot(
        up_lowrank, adapter_up_output, preferred_element_type=jnp.float32
    )
    sigmoid_gate = jax.nn.sigmoid(gate_signal)
    activated = gate_signal * sigmoid_gate
    hidden_state = (activated * up_activation).astype(jnp.bfloat16)
    lowrank_reverse = (member_choose * lowrank_down).astype(jnp.bfloat16)
    hidden_gradient = frozen_gradient + jnp.einsum(
        "os,ns->on", lowrank_reverse, adapter_down_input, preferred_element_type=jnp.float32
    )
    grad_gate = (
        hidden_gradient * up_activation * sigmoid_gate * (1.0 + gate_signal * (1.0 - sigmoid_gate))
    ).astype(jnp.bfloat16)
    up_gradient = (hidden_gradient * activated).astype(jnp.bfloat16)
    return (hidden_state, grad_gate, up_gradient, up_lowrank, lowrank_reverse)


def per_device(
    tokens,
    cotangent,
    adapter_index,
    retain_mask,
    gate_weight,
    up_weight,
    down_weight,
    adapter_up_input,
    adapter_up_output,
    adapter_down_input,
    adapter_down_output,
):
    gate_kept = pruned(gate_weight, retain_mask, 0)
    up_retained = pruned(up_weight, retain_mask, 1)
    down_retained = pruned(down_weight, retain_mask, 2)
    own_rows = tokens.shape[0]
    every_token, every_cotangent = (
        lax.all_gather(tokens, "col", axis=0, tiled=True),
        lax.all_gather(cotangent, "col", axis=0, tiled=True),
    )
    columns = jnp.arange(REWARD_ADAPTERS * ADAPTER_RANK, dtype=jnp.int32) // ADAPTER_RANK
    member_choose = (adapter_index[:, None] == columns[None, :]).astype(jnp.float32)
    gate_part = jnp.einsum("td,fd->tf", every_token, gate_kept, preferred_element_type=jnp.float32)
    up_part = jnp.einsum("td,fd->tf", every_token, up_retained, preferred_element_type=jnp.float32)
    lowrank_up_piece = jnp.dot(every_token, adapter_up_input, preferred_element_type=jnp.float32)
    grad_part = jnp.einsum(
        "td,fd->tf", every_cotangent, down_retained, preferred_element_type=jnp.float32
    )
    rank_down_part = jnp.einsum(
        "pe,ue->pu", every_cotangent, adapter_down_output, preferred_element_type=jnp.float32
    )
    reduced_total = (
        lax.psum(gate_part.astype(jnp.bfloat16), "row").astype(jnp.float32),
        lax.psum(up_part.astype(jnp.bfloat16), "row").astype(jnp.float32),
        lax.psum(lowrank_up_piece.astype(jnp.bfloat16), "row").astype(jnp.float32),
        lax.psum(grad_part.astype(jnp.bfloat16), "row").astype(jnp.float32),
        lax.psum(rank_down_part.astype(jnp.bfloat16), "row").astype(jnp.float32),
    )
    hidden_state, grad_gate, up_gradient, up_lowrank, lowrank_reverse = hidden_update(
        reduced_total[0],
        reduced_total[1],
        reduced_total[2],
        reduced_total[3],
        reduced_total[4],
        member_choose,
        adapter_up_output,
        adapter_down_input,
    )
    frozen_output = lax.psum_scatter(
        jnp.dot(hidden_state, down_retained, preferred_element_type=jnp.float32).astype(
            jnp.bfloat16
        ),
        "col",
        scatter_dimension=0,
        tiled=True,
    ).astype(jnp.float32)
    frozen_input = lax.psum_scatter(
        (
            jnp.dot(grad_gate, gate_kept, preferred_element_type=jnp.float32)
            + jnp.dot(up_gradient, up_retained, preferred_element_type=jnp.float32)
        ).astype(jnp.bfloat16),
        "col",
        scatter_dimension=0,
        tiled=True,
    ).astype(jnp.float32)
    down_lowrank_piece = jnp.dot(
        hidden_state, adapter_down_input, preferred_element_type=jnp.float32
    )
    rank_grad_part = jnp.einsum(
        "xl,gl->xg", up_gradient, adapter_up_output, preferred_element_type=jnp.float32
    )
    own_first = lax.axis_index("col") * own_rows
    down_full, grad_full = (
        lax.psum(down_lowrank_piece.astype(jnp.bfloat16), "col").astype(jnp.float32),
        lax.psum(rank_grad_part.astype(jnp.bfloat16), "col").astype(jnp.float32),
    )
    down_lowrank = (member_choose * down_full).astype(jnp.bfloat16)
    lowrank_gradient = (member_choose * grad_full).astype(jnp.bfloat16)
    member_down = lax.dynamic_slice_in_dim(down_lowrank, own_first, own_rows, 0)
    member_gradient = lax.dynamic_slice_in_dim(lowrank_gradient, own_first, own_rows, 0)
    grad_up_in = jnp.dot(every_token.T, lowrank_gradient, preferred_element_type=jnp.float32)
    grad_down_out = jnp.dot(down_lowrank.T, every_cotangent, preferred_element_type=jnp.float32)
    layer_output = (
        frozen_output
        + jnp.dot(member_down, adapter_down_output, preferred_element_type=jnp.float32)
    ).astype(jnp.bfloat16)
    token_gradient = (
        frozen_input
        + jnp.dot(member_gradient, adapter_up_input.T, preferred_element_type=jnp.float32)
    ).astype(jnp.bfloat16)
    grad_up_out = jnp.dot(up_lowrank.T, up_gradient, preferred_element_type=jnp.float32).astype(
        jnp.bfloat16
    )
    grad_down_in = jnp.dot(
        hidden_state.T, lowrank_reverse, preferred_element_type=jnp.float32
    ).astype(jnp.bfloat16)
    return (
        layer_output,
        token_gradient,
        grad_up_in.astype(jnp.bfloat16),
        grad_up_out,
        grad_down_in,
        grad_down_out.astype(jnp.bfloat16),
    )


def solution(mesh):
    return jax.shard_map(
        per_device,
        mesh=mesh,
        in_specs=(
            P(("grp", "col"), "row"),
            P(("grp", "col"), "row"),
            P("grp"),
            P(None, "col", "row"),
            P("col", "row"),
            P("col", "row"),
            P("col", "row"),
            P("row", None),
            P(None, "col"),
            P("col", None),
            P(None, "row"),
        ),
        out_specs=(
            P(("grp", "col"), "row"),
            P(("grp", "col"), "row"),
            P(("grp", "row"), None),
            P("grp", "col"),
            P(("grp", "col"), None),
            P("grp", "row"),
        ),
        check_vma=False,
    )
```

profile of v0, /device:TPU:0, one launch (start us, length us, event | category | flops | bytes accessed | tf_op | source)
XLA Modules:
  0.0 433.8 jit_solution(14992762293649897793)
XLA Ops:
  7.2 0.0 copy-start
  7.2 0.0 all-reduce.7.cloned.1.call-start
  7.2 0.9 convert.5
  8.1 7.2 %mul.69 = bf16[28,64,32,64]{3,2,1,0:T(8,128)(2,1)} broadcast(bf16[28,32]{1,0:T(8,128)(2,1)S(1)} %get-tuple-element.23), dimensions={0,2} | broadcast | bytes 7341824 | tf_op jit(solution)/shard_map/mul | solution.py:15
  15.3 20.8 %mul.70 = bf16[1792,2048]{1,0:T(8,128)(2,1)} reshape(bf16[28,64,32,64]{3,2,1,0:T(8,128)(2,1)} %mul.69) | data formatting | bytes 14680064 | tf_op jit(solution)/shard_map/mul | solution.py:15
  36.1 33.0 %all_gather.6 = bf16[128,2048]{1,0:T(8,128)(2,1)S(1)} all-gather(bf16[16,2048]{1,0:T(8,128)(2,1)S(1)} %copy-done.8), channel_id=1, replica_groups=mesh['grp'=2,'row'=2,'col'=8] {'col'}, dimensions={0}, use_global_device_ids=true | all-gather | bytes 589824 | tf_op jit(solution)/shard_map/all_gather | solution.py:64
  69.1 7.2 %mul.73 = bf16[28,64,32,64]{3,2,1,0:T(8,128)(2,1)} broadcast(bf16[28,32]{1,0:T(8,128)(2,1)S(1)} %get-tuple-element.22), dimensions={0,2} | broadcast | bytes 7341824 | tf_op jit(solution)/shard_map/mul | solution.py:15
  76.3 20.8 %mul.74 = bf16[1792,2048]{1,0:T(8,128)(2,1)} reshape(bf16[28,64,32,64]{3,2,1,0:T(8,128)(2,1)} %mul.73) | data formatting | bytes 14680064 | tf_op jit(solution)/shard_map/mul | solution.py:15
  97.1 7.2 %mul.78 = bf16[28,64,32,64]{3,2,1,0:T(8,128)(2,1)} broadcast(bf16[28,32]{1,0:T(8,128)(2,1)S(1)} %get-tuple-element.21), dimensions={0,2} | broadcast | bytes 7341824 | tf_op jit(solution)/shard_map/mul | solution.py:15
  104.2 20.8 %mul.79 = bf16[1792,2048]{1,0:T(8,128)(2,1)} reshape(bf16[28,64,32,64]{3,2,1,0:T(8,128)(2,1)} %mul.78) | data formatting | bytes 14680064 | tf_op jit(solution)/shard_map/mul | solution.py:15
  125.1 31.5 %all_gather.7 = bf16[128,2048]{1,0:T(8,128)(2,1)S(1)} all-gather(bf16[16,2048]{1,0:T(8,128)(2,1)S(1)} %copy-done.9), channel_id=1, replica_groups=mesh['grp'=2,'row'=2,'col'=8] {'col'}, dimensions={0}, use_global_device_ids=true | all-gather | bytes 589824 | tf_op jit(solution)/shard_map/all_gather | solution.py:65
  156.5 12.5 %mul.71 = bf16[1792,2048]{1,0:T(8,128)(2,1)} multiply(bf16[1792,2048]{1,0:T(8,128)(2,1)} %param.15, bf16[1792,2048]{1,0:T(8,128)(2,1)} %mul.70) | non-fusion elementwise | flops 3670016 | bytes 22020096 | tf_op jit(solution)/shard_map/mul | solution.py:15
  169.1 6.1 %fusion.24 = bf16[128,1792]{0,1:T(8,128)(2,1)} fusion(bf16[1792,2048]{1,0:T(8,128)(2,1)} %mul.71, bf16[128,2048]{1,0:T(8,128)(2,1)S(1)} %all_gather.6), kind=kOutput, calls=%fused_computation.21 | convolution fusion | flops 939753472 | bytes 8323072 | tf_op jit(solution)/shard_map/td,fd->tf/dot_general | solution.py:69
  175.2 0.9 convolution_convert_fusion.8
  176.1 8.6 %fusion.28 = bf16[128,1792]{0,1:T(8,128)(2,1)} fusion(bf16[128,2048]{1,0:T(8,128)(2,1)S(1)} %all_gather.6, bf16[1792,2048]{1,0:T(8,128)(2,1)} %param.16, bf16[1792,2048]{1,0:T(8,128)(2,1)} %mul.74), kind=kOutput, calls=%fused_computation.23 | convolution fusion | flops 943423488 | bytes 15663104 | tf_op jit(solution)/shard_map/td,fd->tf/dot_general | solution.py:70
  184.7 0.0 copy-done.1
  184.8 1.1 convolution_convert_fusion.6
  185.9 0.0 slice-done.1
  185.9 0.0 copy-start.11
  185.9 3.0 fusion.25
  188.9 0.0 all-reduce.7.cloned.1.call-update
  188.9 0.3 all-reduce.5.cloned.1.call-start
  189.2 21.6 %all-reduce.7.cloned.1.call-done = (bf16[128,1792]{0,1:T(8,128)(2,1)}, bf16[128,256]{1,0:T(8,128)(2,1)}, bf16[128,1792]{0,1:T(8,128)(2,1)}, bf16[128,1792]{0,1:T(8,128)(2,1)}, bf16[128,256]{1,0:T(8,128)(2,1)}) async-done(((bf16[128,1792]{0,1:T(8,128)(2,1)}, bf16[128,256]{1,0:T(8,128)(2,1)}, bf16[128,1792]{0,1:T(8,128)(2,1)}, bf16[128,1792]{0,1:T(8,128)(2,1)}, bf16[128,256]{1,0:T(8,128)(2,1)}), ...) | async-done | bytes 1507344 | tf_op jit(solution)/shard_map/psum | solution.py:80
  210.8 2.0 convolution_add_fusion.1
  212.8 0.0 copy-start.5
  212.8 3.2 multiply_convert_fusion
  216.0 0.8 copy-done.2
  216.8 1.1 convolution_convert_fusion.5
  217.9 1.0 convolution_convert_fusion.7
  218.9 6.2 %fusion.39 = f32[128,2048]{1,0:T(8,128)} fusion(bf16[1792,2048]{1,0:T(8,128)(2,1)} %mul.71, bf16[128,1792]{0,1:T(8,128)(2,1)} %get-tuple-element.16, f32[128,1792]{0,1:T(8,128)} %get-tuple-element.26, f32[128,1792]{0,1:T(8,128)} %copy-done.5), kind=kOutput, calls=%fused_computation.43 | convolution fusion | flops 942047232 | bytes 10682368 | tf_op jit(solution)/shard_map/dot_general | solution.py:105
  225.0 0.0 all-reduce.5.cloned.1.call-update
  225.1 0.0 reduce-scatter.5.cloned.1.call-start
  225.1 8.0 %fusion.12 = bf16[128,2048]{1,0:T(8,128)(2,1)} fusion(f32[128,2048]{1,0:T(8,128)} %fusion.39, bf16[128,1792]{0,1:T(8,128)(2,1)} %copy-done.2, bf16[1792,2048]{1,0:T(8,128)(2,1)} %param.16, bf16[1792,2048]{1,0:T(8,128)(2,1)} %mul.74), kind=kOutput, calls=%fused_computation.16 | convolution fusion | flops 943718400 | bytes 16711680 | tf_op jit(solution)/shard_map/dot_general | solution.py:106
  233.2 0.0 reduce-scatter.5.cloned.1.call-update
  233.2 0.0 reduce-scatter.3.cloned.1.call-start
  233.3 2.4 convolution_convert_fusion.1
  235.6 7.7 %fusion.18 = bf16[128,2048]{1,0:T(8,128)(2,1)} fusion(bf16[128,1792]{0,1:T(8,128)(2,1)} %copy-done.3, bf16[1792,2048]{1,0:T(8,128)(2,1)} %param.17, bf16[1792,2048]{1,0:T(8,128)(2,1)} %mul.79), kind=kOutput, calls=%fused_computation.18 | convolution fusion | flops 943456256 | bytes 15663104 | tf_op jit(solution)/shard_map/dot_general | solution.py:96
  243.4 0.0 reduce-scatter.3.cloned.1.call-update
  243.4 2.4 convolution_convert_fusion.2
  245.9 50.5 %all-reduce.5.cloned.1.call-done = (bf16[128,256]{1,0:T(8,128)(2,1)}, bf16[128,256]{1,0:T(8,128)(2,1)}) async-done(((bf16[128,256]{1,0:T(8,128)(2,1)}, bf16[128,256]{1,0:T(8,128)(2,1)}), (bf16[128,256]{1,0:T(8,128)(2,1)}, bf16[128,256]{1,0:T(8,128)(2,1)})) %all-reduce.5.cloned.1.call-update) | async-done | bytes 131088 | tf_op jit(solution)/shard_map/psum | solution.py:120
  296.4 1.0 fusion.45
  297.4 1.4 fusion.8
  298.8 2.3 copy.19
  301.1 1.4 convolution_convert_fusion
  302.5 58.5 %reduce-scatter.5.cloned.1.call-done = bf16[16,2048]{1,0:T(8,128)(2,1)} async-done(((bf16[128,2048]{1,0:T(8,128)(2,1)}), bf16[16,2048]{1,0:T(8,128)(2,1)}) %reduce-scatter.5.cloned.1.call-update) | async-done | bytes 65552 | tf_op jit(solution)/shard_map/reduce_scatter | solution.py:103
  361.0 1.9 fusion.32
  362.8 62.7 %reduce-scatter.3.cloned.1.call-done = bf16[16,2048]{1,0:T(8,128)(2,1)} async-done(((bf16[128,2048]{1,0:T(8,128)(2,1)}), bf16[16,2048]{1,0:T(8,128)(2,1)}) %reduce-scatter.3.cloned.1.call-update) | async-done | bytes 65552 | tf_op jit(solution)/shard_map/reduce_scatter | solution.py:95
  425.5 1.7 fusion.31
  (30 shorter events, 0.1 us)
Async XLA Ops:
  7.2 168.0 %copy-start = (bf16[2048,256]{1,0:T(8,128)(2,1)S(1)}, bf16[2048,256]{1,0:T(8,128)(2,1)}, u32[]{:S(2)}) copy-start(bf16[2048,256]{1,0:T(8,128)(2,1)} %param.18) | copy-start | bytes 3145732
  7.2 203.6 %all-reduce.7.cloned.1.call-start = ((), (), s32[]{:S(2)}) async-start(), calls=%async_computation.5 | async-start | bytes 3014656 | tf_op jit(solution)/shard_map/psum | solution.py:80
  15.3 20.8 %copy-start.8 = (bf16[16,2048]{1,0:T(8,128)(2,1)S(1)}, bf16[16,2048]{1,0:T(8,128)(2,1)}, u32[]{:S(2)}) copy-start(bf16[16,2048]{1,0:T(8,128)(2,1)} %param.11) | copy-start | bytes 196612
  104.2 20.8 %copy-start.9 = (bf16[16,2048]{1,0:T(8,128)(2,1)S(1)}, bf16[16,2048]{1,0:T(8,128)(2,1)}, u32[]{:S(2)}) copy-start(bf16[16,2048]{1,0:T(8,128)(2,1)} %param.12) | copy-start | bytes 196612
  169.1 16.8 %slice-start.2 = ((s8[7340032]{0:T(1024)(128)(4,1)}), s8[4194304]{0:T(1024)(128)(4,1)S(1)}, s32[]{:S(2)}) async-start(s8[7340032]{0:T(1024)(128)(4,1)} %bitcast.47), calls=%async_computation.8 | async-start | bytes 8388608
  175.1 10.7 %slice-start = ((s8[7340032]{0:T(1024)(128)(4,1)}), s8[4194304]{0:T(1024)(128)(4,1)S(1)}, s32[]{:S(2)}) async-start(s8[7340032]{0:T(1024)(128)(4,1)} %bitcast.45), calls=%async_computation.6 | async-start | bytes 8388608
  176.1 8.7 %copy-start.1 = (bf16[256,2048]{1,0:T(8,128)(2,1)S(1)}, bf16[256,2048]{1,0:T(8,128)(2,1)}, u32[]{:S(2)}) copy-start(bf16[256,2048]{1,0:T(8,128)(2,1)} %param.21) | copy-start | bytes 3145732
  176.1 9.8 %slice-start.1 = ((s8[7340032]{0:T(1024)(128)(4,1)}), s8[3145728]{0:T(1024)(128)(4,1)S(1)}, s32[]{:S(2)}) async-start(s8[7340032]{0:T(1024)(128)(4,1)} %bitcast.45), calls=%async_computation.7 | async-start | bytes 6291456
  176.1 9.8 %slice-start.3 = ((s8[7340032]{0:T(1024)(128)(4,1)}), s8[3145728]{0:T(1024)(128)(4,1)S(1)}, s32[]{:S(2)}) async-start(s8[7340032]{0:T(1024)(128)(4,1)} %bitcast.47), calls=%async_computation.9 | async-start | bytes 6291456
  185.9 24.9 %copy-start.11 = (s32[128]{0:T(128)S(1)}, s32[128]{0:T(128)}, u32[]{:S(2)}) copy-start(s32[128]{0:T(128)} %param.13) | copy-start | bytes 1540
  188.9 107.5 %all-reduce.5.cloned.1.call-start = ((), (), s32[]{:S(2)}) async-start(), calls=%async_computation.4 | async-start | bytes 262144 | tf_op jit(solution)/shard_map/psum | solution.py:120
  210.8 6.0 %copy-start.4 = (bf16[256,1792]{1,0:T(8,128)(2,1)S(1)}, bf16[256,1792]{1,0:T(8,128)(2,1)}, u32[]{:S(2)}) copy-start(bf16[256,1792]{1,0:T(8,128)(2,1)} %param.19) | copy-start | bytes 2752516
  210.8 7.1 %copy-start.6 = (bf16[1792,256]{1,0:T(8,128)(2,1)S(1)}, bf16[1792,256]{1,0:T(8,128)(2,1)}, u32[]{:S(2)}) copy-start(bf16[1792,256]{1,0:T(8,128)(2,1)} %param.20) | copy-start | bytes 2752516
  212.8 5.1 %copy-start.5 = (f32[128,1792]{0,1:T(8,128)}, f32[128,1792]{0,1:T(8,128)S(1)}, u32[]{:S(2)}) copy-start(f32[128,1792]{0,1:T(8,128)S(1)} %convolution_add_fusion.1) | copy-start | bytes 2752516
  216.0 0.8 copy-start.2
  216.0 1.9 copy-start.3
  225.1 8.2 %copy-start.10 = (bf16[128,256]{1,0:T(8,128)(2,1)S(1)}, bf16[128,256]{1,0:T(8,128)(2,1)}, u32[]{:S(2)}) copy-start(bf16[128,256]{1,0:T(8,128)(2,1)} %get-tuple-element.18) | copy-start | bytes 196612
  225.1 135.9 %reduce-scatter.5.cloned.1.call-start = ((), (), s32[]{:S(2)}) async-start(), calls=%async_computation.3 | async-start | bytes 589824 | tf_op jit(solution)/shard_map/reduce_scatter | solution.py:103
  233.2 192.3 %reduce-scatter.3.cloned.1.call-start = ((), (), s32[]{:S(2)}) async-start(), calls=%async_computation.2 | async-start | bytes 589824 | tf_op jit(solution)/shard_map/reduce_scatter | solution.py:95
  235.6 7.8 %copy-start.7 = (bf16[128,256]{1,0:T(8,128)(2,1)S(1)}, bf16[128,256]{1,0:T(8,128)(2,1)}, u32[]{:S(2)}) copy-start(bf16[128,256]{1,0:T(8,128)(2,1)} %get-tuple-element.15) | copy-start | bytes 196612
Sparse Core Ops, SparseCore 0:
  189.0 21.7 all-reduce.6
  225.2 71.1 all-reduce.4
  299.8 61.1 reduce-scatter.4
  364.5 60.9 reduce-scatter.2
where the time goes:
time: 436 us; the launch traced here: 434 us
  waiting for transfers between devices  193 us (44%)
  local copies, waits for them, and re-layouts  87 us (20%)
  blocking collectives  64.5 us (15%)
  matrix products  60.2 us (14%)
  other arithmetic  14.4 us (3%)
  between operations  13.9 us (3%)
    mul x6, local copies, waits for them, and re-layouts, pruned(): return (tiles * grid[:, None, :, None]).reshape(unit_rows, model_cols)  84 us
    reduce_scatter x1, waiting for transfers between devices, per_device(): lax.psum_scatter(jnp.dot(hidden_state, down_retained, preferred_element_t...  62.7 us
    reduce_scatter x1, waiting for transfers between devices, per_device(): lax.psum_scatter((jnp.dot(grad_gate, gate_kept, preferred_element_type=jn...  58.5 us
    psum x1, waiting for transfers between devices, per_device(): lax.psum(down_lowrank_piece.astype(jnp.bfloat16), 'col').astype(jnp.float32)  50.5 us
    all_gather x1, blocking collectives, per_device(): lax.all_gather(tokens, 'col', axis=0, tiled=True)  33 us
    all_gather x1, blocking collectives, per_device(): lax.all_gather(cotangent, 'col', axis=0, tiled=True)  31.5 us
    psum x1, waiting for transfers between devices, per_device(): lax.psum(up_part.astype(jnp.bfloat16), 'row').astype(jnp.float32)  21.6 us
    mul x1, other arithmetic, pruned(): return (tiles * grid[:, None, :, None]).reshape(unit_rows, model_cols)  12.5 us
  transfers between devices with their start and end apart: 4, of which 4 were waited for; matrix products, arithmetic and copies ran while one was open for 7% of the time, Pallas kernels for 0%

commit v1 on v0

v1 whole, which is shorter than its diff:
```python
import functools

import jax
import jax.numpy as jnp
from jax import lax
from jax.experimental import pallas as pl
from jax.experimental.pallas import tpu as pltpu
from jax.sharding import PartitionSpec as P

BLOCK = 64
ADAPTER_RANK = 32
MESH = pl.DeviceIdType.MESH
BF16 = jnp.bfloat16
F32 = jnp.float32


def mm(a, b, ca, cb):
    return lax.dot_general(a, b, (((ca,), (cb,)), ((), ())), preferred_element_type=F32)


def kernel(
    n,
    tok_ref, cot_ref, index_ref, mask_ref, gate_hbm, up_hbm, down_hbm, ui_hbm, uo_hbm, di_hbm, do_hbm,
    out_ref, tg_ref, gui_ref, guo_ref, gdi_ref, gdo_ref,
    w, ui, uo, di, do, em, sel, xg, ps, pr, rs, rr, ur, rk, hs, rp, rrb, rg, ob, rb,
    w_sem, a_sem, ag_send, ag_recv, row_send, row_recv, rank_send, rank_recv, rg_send, rg_recv, rs_send, rs_recv,
):
    own = tok_ref.shape[0]
    units, width = gate_hbm.shape
    tokens = own * n
    c = lax.axis_index("col")
    r = lax.axis_index("row")
    fc = 256 if units % 256 == 0 else units
    nfc = units // fc
    dc = 512
    ndc = width // dc

    def rows_of(p):
        return pl.ds(pl.multiple_of(p * own, own), own)

    def fch(j):
        return pl.ds(pl.multiple_of(j * fc, fc), fc) if nfc > 1 else slice(None)

    def peers(body):
        def step(k, carry):
            body(lax.rem(c + k, n))
            return carry
        lax.fori_loop(1, n, step, 0)

    def loop(count, body):
        if count == 1:
            body(0)
        else:
            def step(j, carry):
                body(j)
                return carry
            lax.fori_loop(0, count, step, 0)

    mine = rows_of(c)

    def w_copy(k, j):
        return pltpu.make_async_copy((gate_hbm, up_hbm, down_hbm)[k].at[fch(j)], w.at[k, fch(j)], w_sem.at[k, j])

    a_copies = [
        pltpu.make_async_copy(src, dst, a_sem.at[i])
        for i, (src, dst) in enumerate(((ui_hbm, ui), (do_hbm, do), (uo_hbm, uo), (di_hbm, di)))
    ]
    for k in range(3):
        loop(nfc, lambda j, k=k: w_copy(k, j).start())
        if k == 0:
            for copy in a_copies:
                copy.start()

    barrier = pltpu.get_barrier_semaphore()
    peers(lambda p: pl.semaphore_signal(barrier, inc=1, device_id={"col": p}, device_id_type=MESH))
    pl.semaphore_signal(barrier, inc=1, device_id={"row": 1 - r}, device_id_type=MESH)
    xg[0, mine] = tok_ref[...]
    xg[1, mine] = cot_ref[...]
    pl.semaphore_wait(barrier, n)

    def ag(owner, p):
        part = xg.at[:, rows_of(owner)]
        return pltpu.make_async_remote_copy(part, part, ag_send.at[p], ag_recv.at[owner], device_id={"col": p}, device_id_type=MESH)

    peers(lambda p: ag(c, p).start())

    member = lax.broadcasted_iota(jnp.int32, (tokens, sel.shape[1]), 1) // ADAPTER_RANK
    sel[...] = jnp.where(index_ref[...] == member, 1.0, 0.0).astype(F32)
    blocks = mask_ref.shape[2]
    spread = (
        lax.broadcasted_iota(jnp.int32, (blocks, width), 1) // BLOCK
        == lax.broadcasted_iota(jnp.int32, (blocks, width), 0)
    ).astype(F32).astype(BF16)
    for k in range(3):
        em[k] = mm(mask_ref[k].astype(F32).astype(BF16), spread, 1, 0)

    def prune(k, j):
        w_copy(k, j).wait()

        def one(b, carry):
            i = j * (fc // BLOCK) + b
            keep = jnp.broadcast_to(em[k, pl.ds(i, 1), :], (16, width)).astype(BF16)
            for q in range(BLOCK // 16):
                at = pl.ds(pl.multiple_of(i * BLOCK + q * 16, 16), 16)
                w[k, at, :] = w[k, at, :] * keep
            return carry
        lax.fori_loop(0, fc // BLOCK, one, 0)

    for k in range(3):
        loop(nfc, functools.partial(prune, k))
    for copy in a_copies:
        copy.wait()
    peers(lambda p: ag(p, c).wait_recv())

    def row_copy(i, src, dst):
        return pltpu.make_async_remote_copy(src, dst, row_send.at[i], row_recv.at[i], device_id={"row": 1 - r}, device_id_type=MESH)

    rank_x = row_copy(3, rs, rr)
    pre_x = [row_copy(k, ps.at[k], pr.at[k]) for k in range(3)]

    rs[0] = mm(xg[0], ui[...], 1, 0).astype(BF16)
    rs[1] = mm(xg[1], do[...], 1, 1).astype(BF16)
    rank_x.start()
    for k in range(3):
        def pre(j, k=k):
            ps[k, :, fch(j)] = mm(xg[k // 2], w[k, fch(j), :], 1, 1).astype(BF16)
        loop(nfc, pre)
        pre_x[k].start()

    rank_x.wait_recv()
    for i in range(2):
        ur[i] = (sel[...] * (rs[i].astype(F32) + rr[i].astype(F32))).astype(BF16)
    for k in range(3):
        pre_x[k].wait_recv()

    rk[...] = jnp.zeros_like(rk)

    def middle(j):
        f = fch(j)
        gate = ps[0, :, f].astype(F32) + pr[0, :, f].astype(F32)
        up = ps[1, :, f].astype(F32) + pr[1, :, f].astype(F32) + mm(ur[0], uo[:, f], 1, 0)
        back = ps[2, :, f].astype(F32) + pr[2, :, f].astype(F32) + mm(ur[1], di[f, :], 1, 1)
        s = jax.nn.sigmoid(gate)
        act = gate * s
        hidden = (act * up).astype(BF16)
        grad_up = (back * act).astype(BF16)
        hs[0, :, f] = hidden
        hs[1, :, f] = (back * up * s * (1.0 + gate * (1.0 - s))).astype(BF16)
        hs[2, :, f] = grad_up
        rk[0] += mm(hidden, di[f, :], 1, 0)
        rk[1] += mm(grad_up, uo[:, f], 1, 1)

    loop(nfc, middle)
    rp[...] = rk[...].astype(BF16)

    def rank_copy(owner, p):
        return pltpu.make_async_remote_copy(rp.at[:, rows_of(p)], rrb.at[owner], rank_send.at[p], rank_recv.at[owner], device_id={"col": p}, device_id_type=MESH)

    peers(lambda p: rank_copy(c, p).start())
    rrb[c] = rp[:, mine]

    def share(i, owner, p):
        return pltpu.make_async_remote_copy(ob.at[i, rows_of(p)], rb.at[i, owner], rs_send.at[i, p], rs_recv.at[i, owner], device_id={"col": p}, device_id_type=MESH)

    def dch(j):
        return pl.ds(pl.multiple_of(j * dc, dc), dc)

    def grad_share(j):
        d = dch(j)
        ob[1, :, d] = (mm(hs[1], w[0, :, d], 1, 0) + mm(hs[2], w[1, :, d], 1, 0)).astype(BF16)

    loop(ndc, grad_share)
    peers(lambda p: share(1, c, p).start())
    rb[1, c] = ob[1, mine]

    peers(lambda p: rank_copy(p, c).wait_recv())
    summed = jnp.zeros(rrb.shape[1:], F32)
    summed = lax.fori_loop(0, n, lambda q, acc: acc + rrb[q].astype(F32), summed)
    rg[:, mine] = (sel[mine, :][None] * summed).astype(BF16)

    def rg_copy(owner, p):
        part = rg.at[:, rows_of(owner)]
        return pltpu.make_async_remote_copy(part, part, rg_send.at[p], rg_recv.at[owner], device_id={"col": p}, device_id_type=MESH)

    peers(lambda p: rg_copy(c, p).start())

    def out_share(j):
        d = dch(j)
        ob[0, :, d] = mm(hs[0], w[2, :, d], 1, 0).astype(BF16)

    loop(ndc, out_share)
    peers(lambda p: share(0, c, p).start())
    rb[0, c] = ob[0, mine]

    def local_grads(j):
        f = fch(j)
        guo_ref[:, f] = mm(ur[0], hs[2, :, f], 0, 0).astype(BF16)
        gdi_ref[f, :] = mm(hs[0, :, f], ur[1], 0, 0).astype(BF16)

    loop(nfc, local_grads)
    peers(lambda p: rg_copy(p, c).wait_recv())

    def rank_grads(j):
        d = dch(j)
        gui_ref[d, :] = mm(xg[0, :, d], rg[1], 0, 0).astype(BF16)
        gdo_ref[:, d] = mm(rg[0], xg[1, :, d], 0, 0).astype(BF16)

    loop(ndc, rank_grads)
    peers(lambda p: share(1, p, c).wait_recv())

    def final(i, dest, adapter, contract):
        def step(j):
            d = dch(j)
            total = jnp.zeros((own, dc), F32)
            total = lax.fori_loop(0, n, lambda q, acc: acc + rb[i, q, :, d].astype(F32), total)
            side = adapter[:, d] if contract == 0 else adapter[d, :]
            dest[:, d] = (total + mm(rg[i, mine], side, 1, contract)).astype(BF16)
        loop(ndc, step)

    final(1, tg_ref, ui, 1)
    peers(lambda p: share(0, p, c).wait_recv())
    final(0, out_ref, do, 0)

    rank_x.wait_send()
    for k in range(3):
        pre_x[k].wait_send()

    def drain(p):
        ag(c, p).wait_send()
        rank_copy(c, p).wait_send()
        rg_copy(c, p).wait_send()
        share(0, c, p).wait_send()
        share(1, c, p).wait_send()
    peers(drain)


def per_device(n, tokens, cotangent, adapter_index, retain_mask, gate_weight, up_weight, down_weight, ui, uo, di, do):
    own, width = tokens.shape
    units = gate_weight.shape[0]
    ranks = ui.shape[1]
    group = own * n
    nfc = units // 256 if units % 256 == 0 else 1
    vmem = pl.BlockSpec(memory_space=pltpu.VMEM)
    hbm = pl.BlockSpec(memory_space=pl.ANY)
    dma = pltpu.SemaphoreType.DMA
    V = pltpu.VMEM
    return pl.pallas_call(
        functools.partial(kernel, n),
        out_shape=tuple(
            jax.ShapeDtypeStruct(s, BF16)
            for s in ((own, width), (own, width), (width, ranks), (ranks, units), (units, ranks), (ranks, width))
        ),
        in_specs=[vmem] * 4 + [hbm] * 7,
        out_specs=tuple([vmem] * 6),
        scratch_shapes=[
            V((3, units, width), BF16), V((width, ranks), BF16), V((ranks, units), BF16), V((units, ranks), BF16), V((ranks, width), BF16),
            V((3, units // BLOCK, width), F32), V((group, ranks), F32), V((2, group, width), BF16),
            V((3, group, units), BF16), V((3, group, units), BF16), V((2, group, ranks), BF16), V((2, group, ranks), BF16),
            V((2, group, ranks), BF16), V((2, group, ranks), F32), V((3, group, units), BF16),
            V((2, group, ranks), BF16), V((n, 2, own, ranks), BF16), V((2, group, ranks), BF16),
            V((2, group, width), BF16), V((2, n, own, width), BF16),
            dma((3, nfc)), dma((4,)), dma((n,)), dma((n,)), dma((4,)), dma((4,)), dma((n,)), dma((n,)), dma((n,)), dma((n,)), dma((2, n)), dma((2, n)),
        ],
        compiler_params=pltpu.CompilerParams(collective_id=0, has_side_effects=True, vmem_limit_bytes=58 * 1024 * 1024),
    )(tokens, cotangent, adapter_index.reshape(group, 1), retain_mask, gate_weight, up_weight, down_weight, ui, uo, di, do)


def solution(mesh):
    return jax.shard_map(
        functools.partial(per_device, mesh.shape["col"]),
        mesh=mesh,
        in_specs=(
            P(("grp", "col"), "row"),
            P(("grp", "col"), "row"),
            P("grp"),
            P(None, "col", "row"),
            P("col", "row"),
            P("col", "row"),
            P("col", "row"),
            P("row", None),
            P(None, "col"),
            P("col", None),
            P(None, "row"),
        ),
        out_specs=(
            P(("grp", "col"), "row"),
            P(("grp", "col"), "row"),
            P(("grp", "row"), None),
            P("grp", "col"),
            P(("grp", "col"), None),
            P("grp", "row"),
        ),
        check_vma=False,
    )
```

time: 436 us -> 89.6 us (0.21)
  the two profiles are of different devices: /device:TPU:0 before, /device:TPU:29 now
where the time goes in v1:
time: 89.6 us; the launch traced here: 89.2 us
  Pallas kernels  75.3 us (84%)
  local copies, waits for them, and re-layouts  13.2 us (15%)
    pallas_call x1, Pallas kernels, per_device(): pl.pallas_call(functools.partial(kernel, n), out_shape=tuple((jax.ShapeDt...  75.3 us
    unnamed x6, local copies, waits for them, and re-layouts  11.8 us

profile of v1, /device:TPU:29, one launch (start us, length us, event | category | flops | bytes accessed | tf_op | source)
XLA Modules:
  0.0 89.2 jit_solution(8158910002509711007)
XLA Ops:
  0.6 1.4 %copy.17.index_ref = s32[128,1]{1,0:T(8,128)} copy(s32[128,1]{0,1:T(1,128)} %bitcast.1) | data formatting | bytes 1024 | tf_op jit(solution)/shard_map/reshape | solution.py:265
  2.0 75.3 %shard_map.154 = (bf16[16,2048]{1,0:T(8,128)(2,1)}, bf16[16,2048]{1,0:T(8,128)(2,1)}, bf16[2048,256]{1,0:T(8,128)(2,1)}, bf16[256,1792]{1,0:T(8,128)(2,1)}, bf16...) custom-call(bf16[16,2048]{1,0:T(8,128)(2,1)} %tok_ref.1, bf16[16,2048]{1,0:T(8,128)(2,1)} %cot_ref.1, ...), custom_call_target="tpu_custom_call" | custom-call | tf_op jit(solution)/shard_map/pallas_call | solution.py:247
  77.4 1.5 %copy.24 = bf16[16,2048]{1,0:T(8,128)(2,1)} copy(bf16[16,2048]{1,0:T(8,128)(2,1)} %get-tuple-element.12) | data formatting | bytes 131072
  78.8 1.5 %copy.25 = bf16[16,2048]{1,0:T(8,128)(2,1)} copy(bf16[16,2048]{1,0:T(8,128)(2,1)} %get-tuple-element.13) | data formatting | bytes 131072
  80.3 2.3 %copy.26 = bf16[2048,256]{1,0:T(8,128)(2,1)} copy(bf16[2048,256]{1,0:T(8,128)(2,1)} %get-tuple-element.14) | data formatting | bytes 2097152
  82.6 2.2 %copy.27 = bf16[256,1792]{1,0:T(8,128)(2,1)} copy(bf16[256,1792]{1,0:T(8,128)(2,1)} %get-tuple-element.15) | data formatting | bytes 1835008
  84.7 2.2 %copy.28 = bf16[1792,256]{1,0:T(8,128)(2,1)} copy(bf16[1792,256]{1,0:T(8,128)(2,1)} %get-tuple-element.16) | data formatting | bytes 1835008
  86.9 2.3 %copy.29 = bf16[256,2048]{1,0:T(8,128)(2,1)} copy(bf16[256,2048]{1,0:T(8,128)(2,1)} %get-tuple-element.17) | data formatting | bytes 2097152

commit v2 on v1

--- a/solution.py
+++ b/solution.py
@@ -22,14 +22,18 @@
     n,
     tok_ref, cot_ref, index_ref, mask_ref, gate_hbm, up_hbm, down_hbm, ui_hbm, uo_hbm, di_hbm, do_hbm,
     out_ref, tg_ref, gui_ref, guo_ref, gdi_ref, gdo_ref,
-    w, ui, uo, di, do, em, sel, xg, ps, pr, rs, rr, ur, rk, hs, rp, rrb, rg, ob, rb,
-    w_sem, a_sem, ag_send, ag_recv, row_send, row_recv, rank_send, rank_recv, rg_send, rg_recv, rs_send, rs_recv,
+    w, ui, uo, di, do, em, sel, xg, ps, pr, rs, rr, ur, rk, hs, rp, rrb, rg, ob, ya, s2, rb,
+    w_sem, a_sem, ag_send, ag_recv, row_send, row_recv, rank_send, rank_recv, rg_send, rg_recv, ra_send, ra_recv, rs_send, rs_recv,
 ):
     own = tok_ref.shape[0]
     units, width = gate_hbm.shape
     tokens = own * n
     c = lax.axis_index("col")
     r = lax.axis_index("row")
+    half = n // 2
+    z, y = c // 2, lax.rem(c, 2)
+    other = 1 - y
+    partner = 2 * z + other
     fc = 256 if units % 256 == 0 else units
     nfc = units // fc
     dc = 512
@@ -55,6 +59,12 @@
                 body(j)
                 return carry
             lax.fori_loop(0, count, step, 0)
+
+    def lines(body, first=1, last=None):
+        def step(k, carry):
+            body(lax.rem(z + k, half))
+            return carry
+        lax.fori_loop(first, half if last is None else last, step, 0)
 
     mine = rows_of(c)
 
@@ -78,14 +88,19 @@
     xg[1, mine] = cot_ref[...]
     pl.semaphore_wait(barrier, n)
 
-    def ag(owner, p):
+    def ag(owner, p, slot):
         part = xg.at[:, rows_of(owner)]
-        return pltpu.make_async_remote_copy(part, part, ag_send.at[p], ag_recv.at[owner], device_id={"col": p}, device_id_type=MESH)
-
-    peers(lambda p: ag(c, p).start())
-
-    member = lax.broadcasted_iota(jnp.int32, (tokens, sel.shape[1]), 1) // ADAPTER_RANK
-    sel[...] = jnp.where(index_ref[...] == member, 1.0, 0.0).astype(F32)
+        return pltpu.make_async_remote_copy(part, part, ag_send.at[slot], ag_recv.at[owner], device_id={"col": p}, device_id_type=MESH)
+
+    lines(lambda q: ag(c, 2 * q + y, 2 * q + y).start())
+    ag(c, partner, partner).start()
+
+    def forward(q):
+        ag(2 * q + y, c, c).wait_recv()
+        ag(2 * q + y, partner, 2 * q + other).start()
+
+    member = lax.broadcasted_iota(jnp.int32, (sel.shape[1], tokens), 0) // ADAPTER_RANK
+    sel[...] = jnp.where(index_ref[...] == member, 1.0, 0.0).astype(F32).T
     blocks = mask_ref.shape[2]
     spread = (
         lax.broadcasted_iota(jnp.int32, (blocks, width), 1) // BLOCK
@@ -108,35 +123,37 @@
 
     for k in range(3):
         loop(nfc, functools.partial(prune, k))
+        lines(forward, 1 + (half - 1) * k // 3, 1 + (half - 1) * (k + 1) // 3)
     for copy in a_copies:
         copy.wait()
-    peers(lambda p: ag(p, c).wait_recv())
+    ag(partner, c, c).wait_recv()
+    lines(lambda q: ag(2 * q + other, c, c).wait_recv())
 
     def row_copy(i, src, dst):
         return pltpu.make_async_remote_copy(src, dst, row_send.at[i], row_recv.at[i], device_id={"row": 1 - r}, device_id_type=MESH)
 
-    rank_x = row_copy(3, rs, rr)
-    pre_x = [row_copy(k, ps.at[k], pr.at[k]) for k in range(3)]
+    rank_x = row_copy(nfc, rs, rr)
+
+    def pre_x(j):
+        return row_copy(j, ps.at[:, :, fch(j)], pr.at[:, :, fch(j)])
 
     rs[0] = mm(xg[0], ui[...], 1, 0).astype(BF16)
     rs[1] = mm(xg[1], do[...], 1, 1).astype(BF16)
     rank_x.start()
-    for k in range(3):
-        def pre(j, k=k):
+    def pre(j):
+        for k in range(3):
             ps[k, :, fch(j)] = mm(xg[k // 2], w[k, fch(j), :], 1, 1).astype(BF16)
-        loop(nfc, pre)
-        pre_x[k].start()
-
+        pre_x(j).start()
+
+    loop(nfc, pre)
     rank_x.wait_recv()
     for i in range(2):
         ur[i] = (sel[...] * (rs[i].astype(F32) + rr[i].astype(F32))).astype(BF16)
-    for k in range(3):
-        pre_x[k].wait_recv()
-
     rk[...] = jnp.zeros_like(rk)
 
     def middle(j):
         f = fch(j)
+        pre_x(j).wait_recv()
         gate = ps[0, :, f].astype(F32) + pr[0, :, f].astype(F32)
         up = ps[1, :, f].astype(F32) + pr[1, :, f].astype(F32) + mm(ur[0], uo[:, f], 1, 0)
         back = ps[2, :, f].astype(F32) + pr[2, :, f].astype(F32) + mm(ur[1], di[f, :], 1, 1)
@@ -159,8 +176,26 @@
     peers(lambda p: rank_copy(c, p).start())
     rrb[c] = rp[:, mine]
 
-    def share(i, owner, p):
-        return pltpu.make_async_remote_copy(ob.at[i, rows_of(p)], rb.at[i, owner], rs_send.at[i, p], rs_recv.at[i, owner], device_id={"col": p}, device_id_type=MESH)
+    def to_partner(i, q):
+        return pltpu.make_async_remote_copy(ob.at[i, rows_of(2 * q + other)], ya.at[i, q], ra_send.at[i, q], ra_recv.at[i, q], device_id={"col": partner}, device_id_type=MESH)
+
+    def along(i, q, owner):
+        return pltpu.make_async_remote_copy(s2.at[i, q], rb.at[i, owner], rs_send.at[i, q], rs_recv.at[i, owner], device_id={"col": 2 * q + y}, device_id_type=MESH)
+
+    def first_hop(i):
+        lines(lambda q: to_partner(i, q).start())
+        to_partner(i, z).start()
+
+    def pair_sum(i, q):
+        to_partner(i, q).wait_recv()
+        return (ob[i, rows_of(2 * q + y)].astype(F32) + ya[i, q].astype(F32)).astype(BF16)
+
+    def second_hop(i):
+        def go(q):
+            s2[i, q] = pair_sum(i, q)
+            along(i, q, z).start()
+        lines(go)
+        rb[i, z] = pair_sum(i, z)
 
     def dch(j):
         return pl.ds(pl.multiple_of(j * dc, dc), dc)
@@ -169,10 +204,12 @@
         d = dch(j)
         ob[1, :, d] = (mm(hs[1], w[0, :, d], 1, 0) + mm(hs[2], w[1, :, d], 1, 0)).astype(BF16)
 
-    loop(ndc, grad_share)
-    peers(lambda p: share(1, c, p).start())
-    rb[1, c] = ob[1, mine]
-
+    def out_share(j):
+        d = dch(j)
+        ob[0, :, d] = mm(hs[0], w[2, :, d], 1, 0).astype(BF16)
+
+    loop(ndc, out_share)
+    first_hop(0)
     peers(lambda p: rank_copy(p, c).wait_recv())
     summed = jnp.zeros(rrb.shape[1:], F32)
     summed = lax.fori_loop(0, n, lambda q, acc: acc + rrb[q].astype(F32), summed)
@@ -184,13 +221,9 @@
 
     peers(lambda p: rg_copy(c, p).start())
 
-    def out_share(j):
-        d = dch(j)
-        ob[0, :, d] = mm(hs[0], w[2, :, d], 1, 0).astype(BF16)
-
-    loop(ndc, out_share)
-    peers(lambda p: share(0, c, p).start())
-    rb[0, c] = ob[0, mine]
+    loop(ndc, grad_share)
+    first_hop(1)
+    second_hop(0)
 
     def local_grads(j):
         f = fch(j)
@@ -198,6 +231,7 @@
         gdi_ref[f, :] = mm(hs[0, :, f], ur[1], 0, 0).astype(BF16)
 
     loop(nfc, local_grads)
+    second_hop(1)
     peers(lambda p: rg_copy(p, c).wait_recv())
 
     def rank_grads(j):
@@ -206,32 +240,49 @@
         gdo_ref[:, d] = mm(rg[0], xg[1, :, d], 0, 0).astype(BF16)
 
     loop(ndc, rank_grads)
-    peers(lambda p: share(1, p, c).wait_recv())
 
     def final(i, dest, adapter, contract):
         def step(j):
             d = dch(j)
             total = jnp.zeros((own, dc), F32)
-            total = lax.fori_loop(0, n, lambda q, acc: acc + rb[i, q, :, d].astype(F32), total)
+            total = lax.fori_loop(0, half, lambda q, acc: acc + rb[i, q, :, d].astype(F32), total)
             side = adapter[:, d] if contract == 0 else adapter[d, :]
             dest[:, d] = (total + mm(rg[i, mine], side, 1, contract)).astype(BF16)
         loop(ndc, step)
 
+    lines(lambda q: along(0, z, q).wait_recv())
+    final(0, out_ref, do, 0)
+    lines(lambda q: along(1, z, q).wait_recv())
     final(1, tg_ref, ui, 1)
-    peers(lambda p: share(0, p, c).wait_recv())
-    final(0, out_ref, do, 0)
 
     rank_x.wait_send()
-    for k in range(3):
-        pre_x[k].wait_send()
+    loop(nfc, lambda j: pre_x(j).wait_send())
+    ag(c, partner, partner).wait_send()
+
+    def drain_lines(q):
+        ag(c, 2 * q + y, 2 * q + y).wait_send()
+        ag(2 * q + y, partner, 2 * q + other).wait_send()
+        for i in range(2):
+            to_partner(i, q).wait_send()
+            along(i, q, z).wait_send()
+    lines(drain_lines)
+    for i in range(2):
+        to_partner(i, z).wait_send()
 
     def drain(p):
-        ag(c, p).wait_send()
         rank_copy(c, p).wait_send()
         rg_copy(c, p).wait_send()
-        share(0, c, p).wait_send()
-        share(1, c, p).wait_send()
     peers(drain)
+
+
+def store(*refs):
+    count = len(refs) // 2
+    sems = refs[-1]
+    copies = [pltpu.make_async_copy(refs[i], refs[count + i], sems.at[i]) for i in range(count)]
+    for copy in copies:
+        copy.start()
+    for copy in copies:
+        copy.wait()
 
 
 def per_device(n, tokens, cotangent, adapter_index, retain_mask, gate_weight, up_weight, down_weight, ui, uo, di, do):
@@ -244,12 +295,13 @@
     hbm = pl.BlockSpec(memory_space=pl.ANY)
     dma = pltpu.SemaphoreType.DMA
     V = pltpu.VMEM
-    return pl.pallas_call(
+    shapes = tuple(
+        jax.ShapeDtypeStruct(s, BF16)
+        for s in ((own, width), (own, width), (width, ranks), (ranks, units), (units, ranks), (ranks, width))
+    )
+    held = pl.pallas_call(
         functools.partial(kernel, n),
-        out_shape=tuple(
-            jax.ShapeDtypeStruct(s, BF16)
-            for s in ((own, width), (own, width), (width, ranks), (ranks, units), (units, ranks), (ranks, width))
-        ),
+        out_shape=tuple(V(s.shape, BF16) for s in shapes),
         in_specs=[vmem] * 4 + [hbm] * 7,
         out_specs=tuple([vmem] * 6),
         scratch_shapes=[
@@ -258,11 +310,20 @@
             V((3, group, units), BF16), V((3, group, units), BF16), V((2, group, ranks), BF16), V((2, group, ranks), BF16),
             V((2, group, ranks), BF16), V((2, group, ranks), F32), V((3, group, units), BF16),
             V((2, group, ranks), BF16), V((n, 2, own, ranks), BF16), V((2, group, ranks), BF16),
-            V((2, group, width), BF16), V((2, n, own, width), BF16),
-            dma((3, nfc)), dma((4,)), dma((n,)), dma((n,)), dma((4,)), dma((4,)), dma((n,)), dma((n,)), dma((n,)), dma((n,)), dma((2, n)), dma((2, n)),
+            V((2, group, width), BF16), V((2, n // 2, own, width), BF16), V((2, n // 2, own, width), BF16), V((2, n // 2, own, width), BF16),
+            dma((3, nfc)), dma((4,)), dma((n,)), dma((n,)), dma((nfc + 1,)), dma((nfc + 1,)), dma((n,)), dma((n,)), dma((n,)), dma((n,)),
+            dma((2, n // 2)), dma((2, n // 2)), dma((2, n // 2)), dma((2, n // 2)),
         ],
-        compiler_params=pltpu.CompilerParams(collective_id=0, has_side_effects=True, vmem_limit_bytes=58 * 1024 * 1024),
-    )(tokens, cotangent, adapter_index.reshape(group, 1), retain_mask, gate_weight, up_weight, down_weight, ui, uo, di, do)
+        compiler_params=pltpu.CompilerParams(collective_id=0, has_side_effects=True, vmem_limit_bytes=50 * 1024 * 1024),
+    )(tokens, cotangent, adapter_index.reshape(1, group), retain_mask, gate_weight, up_weight, down_weight, ui, uo, di, do)
+    return pl.pallas_call(
+        store,
+        out_shape=shapes,
+        in_specs=[vmem] * 6,
+        out_specs=tuple([hbm] * 6),
+        scratch_shapes=[dma((6,))],
+        compiler_params=pltpu.CompilerParams(vmem_limit_bytes=8 * 1024 * 1024),
+    )(*(pltpu.with_memory_space_constraint(x, pltpu.VMEM) for x in held))
 
 
 def solution(mesh):

time: 89.6 us -> 65.8 us (0.73)
  the two profiles are of different devices: /device:TPU:29 before, /device:TPU:0 now
where the time goes in v2:
time: 65.8 us; the launch traced here: 65.6 us
  Pallas kernels  63.5 us (97%)
  local copies, waits for them, and re-layouts  1.45 us (2%)
    pallas_call x1, Pallas kernels, per_device(): pl.pallas_call(functools.partial(kernel, n), out_shape=tuple((V(s.shape,...  61.5 us
    pallas_call x1, Pallas kernels, per_device(): pl.pallas_call(store, out_shape=shapes, in_specs=[vmem] * 6, out_specs=tu...  2.02 us
    unnamed x4, local copies, waits for them, and re-layouts  1.45 us

profile of v2, /device:TPU:0, one launch (start us, length us, event | category | flops | bytes accessed | tf_op | source)
XLA Modules:
  0.0 65.6 jit_solution(2905186084402472336)
XLA Ops:
  0.6 0.0 copy-start
  0.6 0.8 %copy-done = s32[3,28,32]{2,1,0:T(8,128)S(1)} copy-done((s32[3,28,32]{2,1,0:T(8,128)S(1)}, s32[3,28,32]{2,1,0:T(8,128)}, u32[]{:S(2)}) %copy-start) | copy-done | bytes 10776
  1.4 0.0 copy-start.1
  1.4 0.7 copy-done.1
  2.1 61.5 %shard_map.154 = (bf16[16,2048]{1,0:T(8,128)(2,1)S(1)}, bf16[16,2048]{1,0:T(8,128)(2,1)S(1)}, bf16[2048,256]{1,0:T(8,128)(2,1)S(1)}, bf16[256,1792]{1,0:T(8,128)...) custom-call(bf16[16,2048]{1,0:T(8,128)(2,1)} %tok_ref.1, bf16[16,2048]{1,0:T(8,128)(2,1)} %cot_ref.1, ...), custom_call_target="tpu_custom_call" | custom-call | tf_op jit(solution)/shard_map/pallas_call | solution.py:302
  63.6 2.0 %shard_map.155 = (bf16[16,2048]{1,0:T(8,128)(2,1)}, bf16[16,2048]{1,0:T(8,128)(2,1)}, bf16[2048,256]{1,0:T(8,128)(2,1)}, bf16[256,1792]{1,0:T(8,128)(2,1)}, bf16...) custom-call(bf16[16,2048]{1,0:T(8,128)(2,1)S(1)} %get-tuple-element.12.refs_0_, ...), custom_call_target="tpu_custom_call" | custom-call | tf_op jit(solution)/shard_map/pallas_call | solution.py:319
Async XLA Ops:
  0.6 0.8 %copy-start = (s32[3,28,32]{2,1,0:T(8,128)S(1)}, s32[3,28,32]{2,1,0:T(8,128)}, u32[]{:S(2)}) copy-start(s32[3,28,32]{2,1,0:T(8,128)} %mask_ref.1) | copy-start | bytes 32260
  1.4 0.7 copy-start.1

commit v3 on v2

--- a/solution.py
+++ b/solution.py
@@ -38,6 +38,7 @@
     nfc = units // fc
     dc = 512
     ndc = width // dc
+    npc = ndc // 2
 
     def rows_of(p):
         return pl.ds(pl.multiple_of(p * own, own), own)
@@ -88,16 +89,23 @@
     xg[1, mine] = cot_ref[...]
     pl.semaphore_wait(barrier, n)
 
-    def ag(owner, p, slot):
-        part = xg.at[:, rows_of(owner)]
-        return pltpu.make_async_remote_copy(part, part, ag_send.at[slot], ag_recv.at[owner], device_id={"col": p}, device_id_type=MESH)
-
-    lines(lambda q: ag(c, 2 * q + y, 2 * q + y).start())
-    ag(c, partner, partner).start()
-
-    def forward(q):
-        ag(2 * q + y, c, c).wait_recv()
-        ag(2 * q + y, partner, 2 * q + other).start()
+    def ag(i, owner, p, slot):
+        part = xg.at[i, rows_of(owner)]
+        return pltpu.make_async_remote_copy(part, part, ag_send.at[i, slot], ag_recv.at[i, owner], device_id={"col": p}, device_id_type=MESH)
+
+    for i in range(2):
+        lines(lambda q, i=i: ag(i, c, 2 * q + y, 2 * q + y).start())
+        ag(i, c, partner, partner).start()
+
+    def forward(i, part, parts):
+        def go(q):
+            ag(i, 2 * q + y, c, c).wait_recv()
+            ag(i, 2 * q + y, partner, 2 * q + other).start()
+        lines(go, 1 + (half - 1) * part // parts, 1 + (half - 1) * (part + 1) // parts)
+
+    def arrive(i):
+        ag(i, partner, c, c).wait_recv()
+        lines(lambda q: ag(i, 2 * q + other, c, c).wait_recv())
 
     member = lax.broadcasted_iota(jnp.int32, (sel.shape[1], tokens), 0) // ADAPTER_RANK
     sel[...] = jnp.where(index_ref[...] == member, 1.0, 0.0).astype(F32).T
@@ -121,31 +129,36 @@
             return carry
         lax.fori_loop(0, fc // BLOCK, one, 0)
 
-    for k in range(3):
-        loop(nfc, functools.partial(prune, k))
-        lines(forward, 1 + (half - 1) * k // 3, 1 + (half - 1) * (k + 1) // 3)
+    def row_copy(i, src, dst):
+        return pltpu.make_async_remote_copy(src, dst, row_send.at[i], row_recv.at[i], device_id={"row": 1 - r}, device_id_type=MESH)
+
+    rank_x = row_copy(3 * nfc, rs, rr)
+
+    def pre_x(k, j):
+        return row_copy(k * nfc + j, ps.at[k, :, fch(j)], pr.at[k, :, fch(j)])
+
+    def pre(k, j):
+        ps[k, :, fch(j)] = mm(xg[k // 2], w[k, fch(j), :], 1, 1).astype(BF16)
+        pre_x(k, j).start()
+
+    loop(nfc, functools.partial(prune, 0))
+    forward(0, 0, 2)
+    loop(nfc, functools.partial(prune, 1))
+    forward(0, 1, 2)
     for copy in a_copies:
         copy.wait()
-    ag(partner, c, c).wait_recv()
-    lines(lambda q: ag(2 * q + other, c, c).wait_recv())
-
-    def row_copy(i, src, dst):
-        return pltpu.make_async_remote_copy(src, dst, row_send.at[i], row_recv.at[i], device_id={"row": 1 - r}, device_id_type=MESH)
-
-    rank_x = row_copy(nfc, rs, rr)
-
-    def pre_x(j):
-        return row_copy(j, ps.at[:, :, fch(j)], pr.at[:, :, fch(j)])
-
+    arrive(0)
+    loop(nfc, functools.partial(pre, 0))
+    forward(1, 0, 2)
+    loop(nfc, functools.partial(prune, 2))
+    forward(1, 1, 2)
+    loop(nfc, functools.partial(pre, 1))
     rs[0] = mm(xg[0], ui[...], 1, 0).astype(BF16)
+    arrive(1)
     rs[1] = mm(xg[1], do[...], 1, 1).astype(BF16)
     rank_x.start()
-    def pre(j):
-        for k in range(3):
-            ps[k, :, fch(j)] = mm(xg[k // 2], w[k, fch(j), :], 1, 1).astype(BF16)
-        pre_x(j).start()
-
-    loop(nfc, pre)
+    loop(nfc, functools.partial(pre, 2))
+
     rank_x.wait_recv()
     for i in range(2):
         ur[i] = (sel[...] * (rs[i].astype(F32) + rr[i].astype(F32))).astype(BF16)
@@ -153,7 +166,8 @@
 
     def middle(j):
         f = fch(j)
-        pre_x(j).wait_recv()
+        for k in range(3):
+            pre_x(k, j).wait_recv()
         gate = ps[0, :, f].astype(F32) + pr[0, :, f].astype(F32)
         up = ps[1, :, f].astype(F32) + pr[1, :, f].astype(F32) + mm(ur[0], uo[:, f], 1, 0)
         back = ps[2, :, f].astype(F32) + pr[2, :, f].astype(F32) + mm(ur[1], di[f, :], 1, 1)
@@ -200,16 +214,20 @@
     def dch(j):
         return pl.ds(pl.multiple_of(j * dc, dc), dc)
 
-    def grad_share(j):
-        d = dch(j)
-        ob[1, :, d] = (mm(hs[1], w[0, :, d], 1, 0) + mm(hs[2], w[1, :, d], 1, 0)).astype(BF16)
-
-    def out_share(j):
-        d = dch(j)
-        ob[0, :, d] = mm(hs[0], w[2, :, d], 1, 0).astype(BF16)
-
-    loop(ndc, out_share)
-    first_hop(0)
+    def part_share(i):
+        def step(j):
+            d, local = dch(j + (i % 2) * npc), dch(j)
+            if i < 2:
+                term = mm(hs[0], w[2, :, d], 1, 0)
+            else:
+                term = mm(hs[1], w[0, :, d], 1, 0) + mm(hs[2], w[1, :, d], 1, 0)
+            ob[i, :, local] = term.astype(BF16)
+        loop(npc, step)
+        first_hop(i)
+
+    part_share(0)
+    part_share(1)
+
     peers(lambda p: rank_copy(p, c).wait_recv())
     summed = jnp.zeros(rrb.shape[1:], F32)
     summed = lax.fori_loop(0, n, lambda q, acc: acc + rrb[q].astype(F32), summed)
@@ -221,9 +239,10 @@
 
     peers(lambda p: rg_copy(c, p).start())
 
-    loop(ndc, grad_share)
-    first_hop(1)
+    part_share(2)
     second_hop(0)
+    part_share(3)
+    second_hop(1)
 
     def local_grads(j):
         f = fch(j)
@@ -231,7 +250,7 @@
         gdi_ref[f, :] = mm(hs[0, :, f], ur[1], 0, 0).astype(BF16)
 
     loop(nfc, local_grads)
-    second_hop(1)
+    second_hop(2)
     peers(lambda p: rg_copy(p, c).wait_recv())
 
     def rank_grads(j):
@@ -240,33 +259,35 @@
         gdo_ref[:, d] = mm(rg[0], xg[1, :, d], 0, 0).astype(BF16)
 
     loop(ndc, rank_grads)
+    second_hop(3)
 
     def final(i, dest, adapter, contract):
-        def step(j):
-            d = dch(j)
+        lines(lambda q: along(i, z, q).wait_recv())
+        for j in range(npc):
+            d, local = pl.ds((j + (i % 2) * npc) * dc, dc), pl.ds(j * dc, dc)
             total = jnp.zeros((own, dc), F32)
-            total = lax.fori_loop(0, half, lambda q, acc: acc + rb[i, q, :, d].astype(F32), total)
+            total = lax.fori_loop(0, half, lambda q, acc, local=local: acc + rb[i, q, :, local].astype(F32), total)
             side = adapter[:, d] if contract == 0 else adapter[d, :]
-            dest[:, d] = (total + mm(rg[i, mine], side, 1, contract)).astype(BF16)
-        loop(ndc, step)
-
-    lines(lambda q: along(0, z, q).wait_recv())
-    final(0, out_ref, do, 0)
-    lines(lambda q: along(1, z, q).wait_recv())
-    final(1, tg_ref, ui, 1)
+            dest[:, d] = (total + mm(rg[i // 2, mine], side, 1, contract)).astype(BF16)
+
+    for i in range(4):
+        final(i, (out_ref, tg_ref)[i // 2], (do, ui)[i // 2], i // 2)
 
     rank_x.wait_send()
-    loop(nfc, lambda j: pre_x(j).wait_send())
-    ag(c, partner, partner).wait_send()
+    for k in range(3):
+        loop(nfc, lambda j, k=k: pre_x(k, j).wait_send())
+    for i in range(2):
+        ag(i, c, partner, partner).wait_send()
 
     def drain_lines(q):
-        ag(c, 2 * q + y, 2 * q + y).wait_send()
-        ag(2 * q + y, partner, 2 * q + other).wait_send()
         for i in range(2):
+            ag(i, c, 2 * q + y, 2 * q + y).wait_send()
+            ag(i, 2 * q + y, partner, 2 * q + other).wait_send()
+        for i in range(4):
             to_partner(i, q).wait_send()
             along(i, q, z).wait_send()
     lines(drain_lines)
-    for i in range(2):
+    for i in range(4):
         to_partner(i, z).wait_send()
 
     def drain(p):
@@ -310,9 +331,9 @@
             V((3, group, units), BF16), V((3, group, units), BF16), V((2, group, ranks), BF16), V((2, group, ranks), BF16),
             V((2, group, ranks), BF16), V((2, group, ranks), F32), V((3, group, units), BF16),
             V((2, group, ranks), BF16), V((n, 2, own, ranks), BF16), V((2, group, ranks), BF16),
-            V((2, group, width), BF16), V((2, n // 2, own, width), BF16), V((2, n // 2, own, width), BF16), V((2, n // 2, own, width), BF16),
-            dma((3, nfc)), dma((4,)), dma((n,)), dma((n,)), dma((nfc + 1,)), dma((nfc + 1,)), dma((n,)), dma((n,)), dma((n,)), dma((n,)),
-            dma((2, n // 2)), dma((2, n // 2)), dma((2, n // 2)), dma((2, n // 2)),
+            V((4, group, width // 2), BF16), V((4, n // 2, own, width // 2), BF16), V((4, n // 2, own, width // 2), BF16), V((4, n // 2, own, width // 2), BF16),
+            dma((3, nfc)), dma((4,)), dma((2, n)), dma((2, n)), dma((3 * nfc + 1,)), dma((3 * nfc + 1,)), dma((n,)), dma((n,)), dma((n,)), dma((n,)),
+            dma((4, n // 2)), dma((4, n // 2)), dma((4, n // 2)), dma((4, n // 2)),
         ],
         compiler_params=pltpu.CompilerParams(collective_id=0, has_side_effects=True, vmem_limit_bytes=50 * 1024 * 1024),
     )(tokens, cotangent, adapter_index.reshape(1, group), retain_mask, gate_weight, up_weight, down_weight, ui, uo, di, do)

time: 65.8 us -> 63 us (0.957)
  Pallas kernels: 63.5 us -> 60.7 us
    pallas_call x1, Pallas kernels: 61.5 us -> 58.7 us  [per_device(): pl.pallas_call(functools.partial(kernel, n), out_shape=tuple((V(s.shape,...]
where the time goes in v3:
time: 63 us; the launch traced here: 62.8 us
  Pallas kernels  60.7 us (96%)
  local copies, waits for them, and re-layouts  1.45 us (2%)
  between operations  0.65 us (1%)
    pallas_call x1, Pallas kernels, per_device(): pl.pallas_call(functools.partial(kernel, n), out_shape=tuple((V(s.shape,...  58.7 us
    pallas_call x1, Pallas kernels, per_device(): pl.pallas_call(store, out_shape=shapes, in_specs=[vmem] * 6, out_specs=tu...  2.02 us
    unnamed x4, local copies, waits for them, and re-layouts  1.45 us

profile of v3, /device:TPU:0, one launch (start us, length us, event | category | flops | bytes accessed | tf_op | source)
XLA Modules:
  0.0 62.8 jit_solution(8037471823837324726)
XLA Ops:
  0.6 0.0 copy-start
  0.6 0.8 %copy-done = s32[3,28,32]{2,1,0:T(8,128)S(1)} copy-done((s32[3,28,32]{2,1,0:T(8,128)S(1)}, s32[3,28,32]{2,1,0:T(8,128)}, u32[]{:S(2)}) %copy-start) | copy-done | bytes 10776
  1.4 0.0 copy-start.1
  1.4 0.7 %copy-done.1 = s32[128]{0:T(128)S(1)} copy-done((s32[128]{0:T(128)S(1)}, s32[128]{0:T(128)}, u32[]{:S(2)}) %copy-start.1) | copy-done | bytes 536
  2.1 58.7 %shard_map.154 = (bf16[16,2048]{1,0:T(8,128)(2,1)S(1)}, bf16[16,2048]{1,0:T(8,128)(2,1)S(1)}, bf16[2048,256]{1,0:T(8,128)(2,1)S(1)}, bf16[256,1792]{1,0:T(8,128)...) custom-call(bf16[16,2048]{1,0:T(8,128)(2,1)} %tok_ref.1, bf16[16,2048]{1,0:T(8,128)(2,1)} %cot_ref.1, ...), custom_call_target="tpu_custom_call" | custom-call | tf_op jit(solution)/shard_map/pallas_call | solution.py:323
  60.8 2.0 %shard_map.155 = (bf16[16,2048]{1,0:T(8,128)(2,1)}, bf16[16,2048]{1,0:T(8,128)(2,1)}, bf16[2048,256]{1,0:T(8,128)(2,1)}, bf16[256,1792]{1,0:T(8,128)(2,1)}, bf16...) custom-call(bf16[16,2048]{1,0:T(8,128)(2,1)S(1)} %get-tuple-element.12.refs_0_, ...), custom_call_target="tpu_custom_call" | custom-call | tf_op jit(solution)/shard_map/pallas_call | solution.py:340
Async XLA Ops:
  0.6 0.8 %copy-start = (s32[3,28,32]{2,1,0:T(8,128)S(1)}, s32[3,28,32]{2,1,0:T(8,128)}, u32[]{:S(2)}) copy-start(s32[3,28,32]{2,1,0:T(8,128)} %mask_ref.1) | copy-start | bytes 32260
  1.4 0.7 %copy-start.1 = (s32[128]{0:T(128)S(1)}, s32[128]{0:T(128)}, u32[]{:S(2)}) copy-start(s32[128]{0:T(128)} %param.13) | copy-start | bytes 1540

commit v4 on v3

--- a/solution.py
+++ b/solution.py
@@ -141,17 +141,17 @@
         ps[k, :, fch(j)] = mm(xg[k // 2], w[k, fch(j), :], 1, 1).astype(BF16)
         pre_x(k, j).start()
 
+    forward(0, 0, 2)
     loop(nfc, functools.partial(prune, 0))
-    forward(0, 0, 2)
+    forward(0, 1, 2)
     loop(nfc, functools.partial(prune, 1))
-    forward(0, 1, 2)
     for copy in a_copies:
         copy.wait()
+    forward(1, 0, 2)
     arrive(0)
     loop(nfc, functools.partial(pre, 0))
-    forward(1, 0, 2)
+    forward(1, 1, 2)
     loop(nfc, functools.partial(prune, 2))
-    forward(1, 1, 2)
     loop(nfc, functools.partial(pre, 1))
     rs[0] = mm(xg[0], ui[...], 1, 0).astype(BF16)
     arrive(1)

time: 63 us -> 62.7 us (level)
  no operation moved by 1% of the time
where the time goes in v4:
time: 62.7 us; the launch traced here: 62.5 us
  Pallas kernels  60.4 us (96%)
  local copies, waits for them, and re-layouts  1.45 us (2%)
  between operations  0.65 us (1%)
    pallas_call x1, Pallas kernels, per_device(): pl.pallas_call(functools.partial(kernel, n), out_shape=tuple((V(s.shape,...  58.4 us
    pallas_call x1, Pallas kernels, per_device(): pl.pallas_call(store, out_shape=shapes, in_specs=[vmem] * 6, out_specs=tu...  2.02 us
    unnamed x4, local copies, waits for them, and re-layouts  1.45 us

profile of v4, /device:TPU:0, one launch (start us, length us, event | category | flops | bytes accessed | tf_op | source)
XLA Modules:
  0.0 62.5 jit_solution(16977999395830490166)
XLA Ops:
  0.6 0.0 copy-start
  0.6 0.8 %copy-done = s32[3,28,32]{2,1,0:T(8,128)S(1)} copy-done((s32[3,28,32]{2,1,0:T(8,128)S(1)}, s32[3,28,32]{2,1,0:T(8,128)}, u32[]{:S(2)}) %copy-start) | copy-done | bytes 10776
  1.4 0.0 copy-start.1
  1.4 0.7 %copy-done.1 = s32[128]{0:T(128)S(1)} copy-done((s32[128]{0:T(128)S(1)}, s32[128]{0:T(128)}, u32[]{:S(2)}) %copy-start.1) | copy-done | bytes 536
  2.1 58.4 %shard_map.154 = (bf16[16,2048]{1,0:T(8,128)(2,1)S(1)}, bf16[16,2048]{1,0:T(8,128)(2,1)S(1)}, bf16[2048,256]{1,0:T(8,128)(2,1)S(1)}, bf16[256,1792]{1,0:T(8,128)...) custom-call(bf16[16,2048]{1,0:T(8,128)(2,1)} %tok_ref.1, bf16[16,2048]{1,0:T(8,128)(2,1)} %cot_ref.1, ...), custom_call_target="tpu_custom_call" | custom-call | tf_op jit(solution)/shard_map/pallas_call | solution.py:323
  60.5 2.0 %shard_map.155 = (bf16[16,2048]{1,0:T(8,128)(2,1)}, bf16[16,2048]{1,0:T(8,128)(2,1)}, bf16[2048,256]{1,0:T(8,128)(2,1)}, bf16[256,1792]{1,0:T(8,128)(2,1)}, bf16...) custom-call(bf16[16,2048]{1,0:T(8,128)(2,1)S(1)} %get-tuple-element.12.refs_0_, ...), custom_call_target="tpu_custom_call" | custom-call | tf_op jit(solution)/shard_map/pallas_call | solution.py:340
Async XLA Ops:
  0.6 0.8 %copy-start = (s32[3,28,32]{2,1,0:T(8,128)S(1)}, s32[3,28,32]{2,1,0:T(8,128)}, u32[]{:S(2)}) copy-start(s32[3,28,32]{2,1,0:T(8,128)} %mask_ref.1) | copy-start | bytes 32260
  1.4 0.7 %copy-start.1 = (s32[128]{0:T(128)S(1)}, s32[128]{0:T(128)}, u32[]{:S(2)}) copy-start(s32[128]{0:T(128)} %param.13) | copy-start | bytes 1540
